TPU v7x, 32 devices: a whole 2x2x4 slice. The times are simulated.
32 devices in a mesh: band: 4 (over y, core), grid: 8 (over z, x).
Axes of the slice: x: 2, y: 2, z: 4, core: 2. Of those that a mesh axis runs over, the one named last changes fastest.
Arguments:
- ground: float32 [4, 128, 128, 128], P('band', 'grid'), may hold values from -6 to 6
- response: float32 [4, 2, 2, 128, 128, 128], P('band', None, None, None, 'grid'), may hold values from -0.6 to 0.6
- kernel_xc: float32 [128, 128, 128], P('grid'), may hold values from -2 to -0.3
Outputs:
- applied: float32 [4, 2, 2, 128, 128, 128], P('band', None, None, None, 'grid')
All inputs are finite; a program needn't handle non-finite values.
Results may differ from a plain program's by a relative error of at most 0.0001.
Values sent between devices are 32-bit elements; how exact they have to be, the bound alone decides.
A program may use at most 64 MiB of HBM per device.

v0:
```python
import math
import jax
import jax.numpy as jnp
from jax import lax
from jax.sharding import PartitionSpec as P

highest = lax.Precision.HIGHEST
spacing = 0.4527
einsum_forms = ("...xyz,xk->...kyz", "...xyz,yk->...xkz", "...xyz,zk->...xyk")


def dft_tables(length):
    positions = jnp.arange(length, dtype=jnp.int32)
    phases = positions[:, None] * positions[None, :] % length
    angles = phases.astype(jnp.float32) * (2.0 * math.pi / length)
    factor = 1.0 / math.sqrt(length)
    return (jnp.cos(angles) * factor, jnp.sin(angles) * factor)


def along(complex_pair, which_axis, tables, direction):
    real_part, imag_part = complex_pair
    cosine, sine_part = tables

    def contract(operand, matrix):
        return jnp.einsum(einsum_forms[which_axis], operand, matrix, precision=highest)

    new_real = contract(real_part, cosine) - direction * contract(imag_part, sine_part)
    new_imag = contract(imag_part, cosine) + direction * contract(real_part, sine_part)
    return (new_real, new_imag)


def signed_freq(positions, length):
    return jnp.where(positions < (length + 1) // 2, positions, positions - length).astype(
        jnp.float32
    )


def coulomb(freq_first, freq_second, freq_third, length):
    squares = (
        freq_first[:, None, None] ** 2
        + freq_second[None, :, None] ** 2
        + freq_third[None, None, :] ** 2
    )
    edge_len = spacing * length
    return jnp.where(
        squares > 0.5, edge_len * edge_len / (math.pi * jnp.maximum(squares, 1.0)), 0.0
    )


def scaled(complex_pair, weights):
    return (complex_pair[0] * weights, complex_pair[1] * weights)


def potential_whole(density, kernel_xc, tables, grid_len):
    wave_values = along(along(density, 1, tables, -1.0), 2, tables, -1.0)
    wave_values = (
        lax.all_to_all(wave_values[0], "grid", split_axis=1, concat_axis=0, tiled=True),
        lax.all_to_all(wave_values[1], "grid", split_axis=1, concat_axis=0, tiled=True),
    )
    wave_values = along(wave_values, 0, tables, -1.0)
    row_count = wave_values[0].shape[1]
    positions = jnp.arange(grid_len, dtype=jnp.int32)
    freq_second = signed_freq(
        lax.axis_index("grid") * row_count + jnp.arange(row_count, dtype=jnp.int32), grid_len
    )
    weights = coulomb(
        signed_freq(positions, grid_len), freq_second, signed_freq(positions, grid_len), grid_len
    )
    wave_values = along(scaled(wave_values, weights), 0, tables, 1.0)
    cell_values = (
        lax.all_to_all(wave_values[0], "grid", split_axis=0, concat_axis=1, tiled=True),
        lax.all_to_all(wave_values[1], "grid", split_axis=0, concat_axis=1, tiled=True),
    )
    cell_values = along(along(cell_values, 1, tables, 1.0), 2, tables, 1.0)
    return (cell_values[0] + kernel_xc * density[0], cell_values[1] + kernel_xc * density[1])


def on_device(ground, response, kernel_xc):
    grid_len = ground.shape[2]
    tables = dft_tables(grid_len)
    wave_values = (response[:, :, 0], response[:, :, 1])
    wave_values = along(along(wave_values, 0, tables, 1.0), 2, tables, 1.0)
    cell_values = (
        lax.all_to_all(wave_values[0], "grid", split_axis=2, concat_axis=3, tiled=True),
        lax.all_to_all(wave_values[1], "grid", split_axis=2, concat_axis=3, tiled=True),
    )
    cell_values = along(cell_values, 1, tables, 1.0)
    dens_real = jnp.sum(ground * (cell_values[0][:, 0] + cell_values[0][:, 1]), axis=0)
    dens_imag = jnp.sum(ground * (cell_values[1][:, 0] - cell_values[1][:, 1]), axis=0)
    density = lax.psum((dens_real, dens_imag), "band")
    pot_real, pot_imag = potential_whole(density, kernel_xc, tables, grid_len)
    prod_real = ground * pot_real
    prod_imag = ground * pot_imag
    fields = (jnp.stack((prod_real, prod_real), axis=1), jnp.stack((prod_imag, -prod_imag), axis=1))
    fields = along(along(fields, 1, tables, -1.0), 2, tables, -1.0)
    wave_out = (
        lax.all_to_all(fields[0], "grid", split_axis=3, concat_axis=2, tiled=True),
        lax.all_to_all(fields[1], "grid", split_axis=3, concat_axis=2, tiled=True),
    )
    wave_out = along(wave_out, 0, tables, -1.0)
    return jnp.stack(wave_out, axis=2)


def solution(mesh):
    return jax.shard_map(
        on_device,
        mesh=mesh,
        in_specs=(
            P("band", "grid", None, None),
            P("band", None, None, None, "grid", None),
            P("grid", None, None),
        ),
        out_specs=P("band", None, None, None, "grid", None),
        check_vma=False,
    )
```

profile of v0, /device:TPU:0, one launch (start us, length us, event | category | flops | bytes accessed | tf_op | source)
XLA Modules:
  0.0 492.5 jit_solution(3142891739396519265)
XLA Ops:
  6.5 2.5 fusion.380
  9.1 2.6 fusion.18
  11.7 2.6 fusion.19
  14.3 2.6 fusion.25
  16.9 2.6 fusion.24
  19.5 2.4 fusion.12
  21.9 2.1 subtract_bitcast_fusion.3
  24.0 2.5 copy.35
  26.6 7.3 %all-to-all-start = ((f32[1,2,128,16,128]{4,3,1,0,2:T(8,128)}), f32[1,2,128,16,128]{4,3,1,0,2:T(8,128)}, u32[]{:S(2)}, u32[]{:S(2)}) async-start(f32[1,2,128,16,128]{4,3,1,0,2:T(8,128)} %copy.35), calls=%async_computation | async-start | bytes 4194304 | tf_op jit(solution)/shard_map/all_to_all | solution.py:84
  33.8 3.7 fusion.10
  37.5 2.1 add_bitcast_fusion.3
  39.7 2.5 copy.39
  42.2 40.0 %all-to-all-done = f32[1,2,128,16,128]{4,3,1,0,2:T(8,128)} async-done(((f32[1,2,128,16,128]{4,3,1,0,2:T(8,128)}), f32[1,2,128,16,128]{4,3,1,0,2:T(8,128)}, u32[]{:S(2)}, u32[]{:S(2)}) %all-to-all-start) | async-done | bytes 2097184 | tf_op jit(solution)/shard_map/all_to_all | solution.py:84
  82.2 4.4 all-to-all-start.1
  88.8 45.5 %all-to-all-done.1 = f32[1,2,128,16,128]{4,3,1,0,2:T(8,128)} async-done(((f32[1,2,128,16,128]{4,3,1,0,2:T(8,128)}), f32[1,2,128,16,128]{4,3,1,0,2:T(8,128)}, u32[]{:S(2)}, u32[]{:S(2)}) %all-to-all-start.1) | async-done | bytes 2097184 | tf_op jit(solution)/shard_map/all_to_all | solution.py:85
  136.2 2.1 fusion.123
  138.3 2.1 fusion.125
  140.4 2.3 add_bitcast_fusion.2
  142.7 2.3 subtract_bitcast_fusion.2
  146.8 50.8 %all-reduce.3.cloned.1.call-done = (f32[16,128,128]{2,1,0:T(8,128)}, f32[16,128,128]{2,1,0:T(8,128)}) async-done(((f32[16,128,128]{2,1,0:T(8,128)}, f32[16,128,128]{2,1,0:T(8,128)}), (f32[16,128,128]{2,1,0:T(8,128)}, f32[16,128,128]{2,1,0:T(8,128)})) %all-reduce.3.cloned.1.call-update) | async-done | bytes 2097168 | tf_op jit(solution)/shard_map/psum | solution.py:90
  197.6 2.6 fusion.111
  208.4 5.5 %all-to-all-start.2 = ((f32[16,128,128]{2,0,1:T(8,128)}), f32[16,128,128]{2,0,1:T(8,128)}, u32[]{:S(2)}, u32[]{:S(2)}) async-start(f32[16,128,128]{2,0,1:T(8,128)} %copy.43), calls=%async_computation.2 | async-start | bytes 2097152 | tf_op jit(solution)/shard_map/all_to_all | solution.py:57
  218.0 21.8 %all-to-all-done.2 = f32[16,128,128]{2,0,1:T(8,128)} async-done(((f32[16,128,128]{2,0,1:T(8,128)}), f32[16,128,128]{2,0,1:T(8,128)}, u32[]{:S(2)}, u32[]{:S(2)}) %all-to-all-start.2) | async-done | bytes 1048608 | tf_op jit(solution)/shard_map/all_to_all | solution.py:57
  239.7 3.8 all-to-all-start.3
  245.0 24.5 %all-to-all-done.3 = f32[16,128,128]{2,0,1:T(8,128)S(1)} async-done(((f32[16,128,128]{2,0,1:T(8,128)}), f32[16,128,128]{2,0,1:T(8,128)S(1)}, u32[]{:S(2)}, u32[]{:S(2)}) %all-to-all-start.3) | async-done | bytes 1048608 | tf_op jit(solution)/shard_map/all_to_all | solution.py:58
  279.3 4.2 all-to-all-start.4
  287.7 21.5 %all-to-all-done.4 = f32[128,16,128]{2,1,0:T(8,128)} async-done(((f32[128,16,128]{2,1,0:T(8,128)}), f32[128,16,128]{2,1,0:T(8,128)}, u32[]{:S(2)}, u32[]{:S(2)}) %all-to-all-start.4) | async-done | bytes 1048608 | tf_op jit(solution)/shard_map/all_to_all | solution.py:71
  309.2 4.0 all-to-all-start.5
  314.5 24.0 %all-to-all-done.5 = f32[128,16,128]{2,1,0:T(8,128)S(1)} async-done(((f32[128,16,128]{2,1,0:T(8,128)}), f32[128,16,128]{2,1,0:T(8,128)S(1)}, u32[]{:S(2)}, u32[]{:S(2)}) %all-to-all-start.5) | async-done | bytes 1048608 | tf_op jit(solution)/shard_map/all_to_all | solution.py:72
  347.7 2.2 fusion
  349.8 2.3 fusion.1
  353.6 2.3 multiply_add_fusion
  355.9 2.3 multiply_subtract_fusion
  358.2 2.1 fusion.4
  360.4 2.1 subtract_bitcast_fusion.1
  362.5 2.7 copy.59
  365.2 4.4 all-to-all-start.6
  369.6 3.7 fusion.2
  373.3 2.1 add_bitcast_fusion.1
  375.5 2.5 copy.63
  378.0 39.4 %all-to-all-done.6 = f32[1,2,16,128,128]{4,2,1,0,3:T(8,128)} async-done(((f32[1,2,16,128,128]{4,2,1,0,3:T(8,128)}), f32[1,2,16,128,128]{4,2,1,0,3:T(8,128)}, u32[]{:S(2)}, u32[]{:S(2)}) %all-to-all-start.6) | async-done | bytes 2097184 | tf_op jit(solution)/shard_map/all_to_all | solution.py:97
  417.4 4.4 all-to-all-start.7
  423.6 45.9 %all-to-all-done.7 = f32[1,2,16,128,128]{4,2,1,0,3:T(8,128)} async-done(((f32[1,2,16,128,128]{4,2,1,0,3:T(8,128)}), f32[1,2,16,128,128]{4,2,1,0,3:T(8,128)}, u32[]{:S(2)}, u32[]{:S(2)}) %all-to-all-start.7) | async-done | bytes 2097184 | tf_op jit(solution)/shard_map/all_to_all | solution.py:98
  471.4 2.1 fusion.117
  473.5 2.1 fusion.119
  475.7 2.3 add_bitcast_fusion
  478.0 2.3 subtract_bitcast_fusion
  480.8 4.4 copy.65
  (59 shorter events, 49.3 us)
Async XLA Ops:
  19.5 2.4 copy-start.1
  26.6 55.6 %all-to-all-start = ((f32[1,2,128,16,128]{4,3,1,0,2:T(8,128)}), f32[1,2,128,16,128]{4,3,1,0,2:T(8,128)}, u32[]{:S(2)}, u32[]{:S(2)}) async-start(f32[1,2,128,16,128]{4,3,1,0,2:T(8,128)} %copy.35), calls=%async_computation | async-start | bytes 4194304 | tf_op jit(solution)/shard_map/all_to_all | solution.py:84
  82.2 52.2 %all-to-all-start.1 = ((f32[1,2,128,16,128]{4,3,1,0,2:T(8,128)}), f32[1,2,128,16,128]{4,3,1,0,2:T(8,128)}, u32[]{:S(2)}, u32[]{:S(2)}) async-start(f32[1,2,128,16,128]{4,3,1,0,2:T(8,128)} %copy.39), calls=%async_computation.1 | async-start | bytes 4194304 | tf_op jit(solution)/shard_map/all_to_all | solution.py:85
  86.5 111.1 %all-reduce.3.cloned.1.call-start = ((), (), s32[]{:S(2)}) async-start(), calls=%async_computation.8 | async-start | bytes 4194304 | tf_op jit(solution)/shard_map/psum | solution.py:90
  142.7 2.3 copy-start.5
  197.6 2.6 copy-start.2
  201.5 2.7 copy-start.3
  208.4 31.3 %all-to-all-start.2 = ((f32[16,128,128]{2,0,1:T(8,128)}), f32[16,128,128]{2,0,1:T(8,128)}, u32[]{:S(2)}, u32[]{:S(2)}) async-start(f32[16,128,128]{2,0,1:T(8,128)} %copy.43), calls=%async_computation.2 | async-start | bytes 2097152 | tf_op jit(solution)/shard_map/all_to_all | solution.py:57
  239.7 29.7 %all-to-all-start.3 = ((f32[16,128,128]{2,0,1:T(8,128)}), f32[16,128,128]{2,0,1:T(8,128)S(1)}, u32[]{:S(2)}, u32[]{:S(2)}) async-start(f32[16,128,128]{2,0,1:T(8,128)} %copy.47), calls=%async_computation.3 | async-start | bytes 2097152 | tf_op jit(solution)/shard_map/all_to_all | solution.py:58
  279.3 29.9 %all-to-all-start.4 = ((f32[128,16,128]{2,1,0:T(8,128)}), f32[128,16,128]{2,1,0:T(8,128)}, u32[]{:S(2)}, u32[]{:S(2)}) async-start(f32[128,16,128]{2,1,0:T(8,128)} %copy.49), calls=%async_computation.4 | async-start | bytes 2097152 | tf_op jit(solution)/shard_map/all_to_all | solution.py:71
  309.2 29.4 %all-to-all-start.5 = ((f32[128,16,128]{2,1,0:T(8,128)}), f32[128,16,128]{2,1,0:T(8,128)S(1)}, u32[]{:S(2)}, u32[]{:S(2)}) async-start(f32[128,16,128]{2,1,0:T(8,128)} %copy.51), calls=%async_computation.5 | async-start | bytes 2097152 | tf_op jit(solution)/shard_map/all_to_all | solution.py:72
  343.8 2.5 copy-start.4
  343.9 2.5 copy-start.6
  343.9 2.5 copy-start.7
  358.2 2.2 copy-start
  365.2 52.2 %all-to-all-start.6 = ((f32[1,2,16,128,128]{4,2,1,0,3:T(8,128)}), f32[1,2,16,128,128]{4,2,1,0,3:T(8,128)}, u32[]{:S(2)}, u32[]{:S(2)}) async-start(f32[1,2,16,128,128]{4,2,1,0,3:T(8,128)} %copy.59), calls=%async_computation.6 | async-start | bytes 4194304 | tf_op jit(solution)/shard_map/all_to_all | solution.py:97
  417.4 52.2 %all-to-all-start.7 = ((f32[1,2,16,128,128]{4,2,1,0,3:T(8,128)}), f32[1,2,16,128,128]{4,2,1,0,3:T(8,128)}, u32[]{:S(2)}, u32[]{:S(2)}) async-start(f32[1,2,16,128,128]{4,2,1,0,3:T(8,128)} %copy.63), calls=%async_computation.7 | async-start | bytes 4194304 | tf_op jit(solution)/shard_map/all_to_all | solution.py:98
Sparse Core Ops, SparseCore 0:
  146.9 50.6 all-reduce.2
where the time goes:
time: 502 us; the launch traced here: 492 us
  waiting for transfers between devices  313 us (62%)
  matrix products  90.1 us (18%)
  starting transfers between devices  38.3 us (8%)
  local copies, waits for them, and re-layouts  33.9 us (7%)
  between operations  14.4 us (3%)
    dot_general x48, matrix products, contract(): jnp.einsum(einsum_forms[which_axis], operand, matrix, precision=highest)  90.1 us
    psum x1, waiting for transfers between devices, on_device(): density = lax.psum((dens_real, dens_imag), 'band')  50.8 us
    all_to_all x1, waiting for transfers between devices, on_device(): lax.all_to_all(fields[1], 'grid', split_axis=3, concat_axis=2, tiled=True)  45.9 us
    all_to_all x1, waiting for transfers between devices, on_device(): lax.all_to_all(wave_values[1], 'grid', split_axis=2, concat_axis=3, tiled...  45.5 us
    all_to_all x1, waiting for transfers between devices, on_device(): lax.all_to_all(wave_values[0], 'grid', split_axis=2, concat_axis=3, tiled...  40 us
    all_to_all x1, waiting for transfers between devices, on_device(): lax.all_to_all(fields[0], 'grid', split_axis=3, concat_axis=2, tiled=True)  39.4 us
    all_to_all x1, waiting for transfers between devices, potential_whole(): lax.all_to_all(wave_values[1], 'grid', split_axis=1, concat_axis=0, tiled...  24.5 us
    all_to_all x1, waiting for transfers between devices, potential_whole(): lax.all_to_all(wave_values[1], 'grid', split_axis=0, concat_axis=1, tiled...  24 us
  transfers between devices with their start and end apart: 9, of which 9 were waited for; matrix products, arithmetic and copies ran while one was open for 6% of the time, Pallas kernels for 0%

commit v1 on v0

--- a/solution.py
+++ b/solution.py
@@ -7,6 +7,22 @@
 highest = lax.Precision.HIGHEST
 spacing = 0.4527
 einsum_forms = ("...xyz,xk->...kyz", "...xyz,yk->...xkz", "...xyz,zk->...xyk")
+
+
+def take_goods_on_mesh(xx, in_dim, tile_in):
+    moved, val2 = (xx.shape[:in_dim], xx.shape[in_dim + 1 :])
+    current_value = xx.reshape(*moved, tile_in, -1, *val2)
+    return jnp.moveaxis(current_value, in_dim, 0)
+
+
+def register_paths(vec, array_dim):
+    vec = jnp.moveaxis(vec, 0, array_dim)
+    block_out = vec.shape
+    return vec.reshape(
+        *block_out[:array_dim],
+        block_out[array_dim] * block_out[array_dim + 1],
+        *block_out[array_dim + 2 :]
+    )
 
 
 def dft_tables(length):
@@ -67,9 +83,25 @@
         signed_freq(positions, grid_len), freq_second, signed_freq(positions, grid_len), grid_len
     )
     wave_values = along(scaled(wave_values, weights), 0, tables, 1.0)
+
+    def replace_the_steps_all(shard_in, chip_axis, here_x, values):
+        high = lax.psum(1, chip_axis)
+        state_now = lax.axis_index(chip_axis)
+        row_out, r2 = (high, state_now)
+        m_next = take_goods_on_mesh(shard_in, here_x, row_out)
+        buffer = [m_next[r2]]
+        m = 1
+        while m < row_out:
+            raw_out = m_next[r2 ^ m]
+            buffer.append(lax.ppermute(raw_out, chip_axis, [(s, s ^ m) for s in range(row_out)]))
+            m += 1
+        tall = jnp.stack(buffer)
+        m_next = tall[r2 ^ jnp.arange(row_out)]
+        return register_paths(m_next, values)
+
     cell_values = (
         lax.all_to_all(wave_values[0], "grid", split_axis=0, concat_axis=1, tiled=True),
-        lax.all_to_all(wave_values[1], "grid", split_axis=0, concat_axis=1, tiled=True),
+        replace_the_steps_all(wave_values[1], "grid", 0, 1),
     )
     cell_values = along(along(cell_values, 1, tables, 1.0), 2, tables, 1.0)
     return (cell_values[0] + kernel_xc * density[0], cell_values[1] + kernel_xc * density[1])

time: 502 us -> 502 us (level)
  starting transfers between devices: 38.3 us -> 49.1 us
  waiting for transfers between devices: 313 us -> 303 us
    ppermute x0 -> x7, waiting for transfers between devices: none -> 34.5 us  [replace_the_steps_all(): lax.ppermute(raw_out, chip_axis, [(s, s ^ m) for s in range(row_out)])]
    all_to_all x1 -> x0, waiting for transfers between devices: 24 us -> none  [potential_whole(): lax.all_to_all(wave_values[1], 'grid', split_axis=0, concat_axis=1, tiled...]
    all_to_all x1, waiting for transfers between devices: 21.5 us -> 0.01 us  [potential_whole(): lax.all_to_all(wave_values[0], 'grid', split_axis=0, concat_axis=1, tiled...]
    ppermute x0 -> x7, starting transfers between devices: none -> 14.1 us  [replace_the_steps_all(): lax.ppermute(raw_out, chip_axis, [(s, s ^ m) for s in range(row_out)])]
  transfers between devices with their start and end apart: 9 -> 15, of which waited for: 9 -> 10; matrix products, arithmetic and copies ran while one was open for 6% -> 6% of each run, Pallas kernels for 0% -> 0%
where the time goes in v1:
time: 502 us; the launch traced here: 492 us
  waiting for transfers between devices  303 us (60%)
  matrix products  90 us (18%)
  starting transfers between devices  49.1 us (10%)
  local copies, waits for them, and re-layouts  33.5 us (7%)
  between operations  14.6 us (3%)
    dot_general x48, matrix products, contract(): jnp.einsum(einsum_forms[which_axis], operand, matrix, precision=highest)  90 us
    psum x1, waiting for transfers between devices, on_device(): density = lax.psum((dens_real, dens_imag), 'band')  50.8 us
    all_to_all x1, waiting for transfers between devices, on_device(): lax.all_to_all(fields[1], 'grid', split_axis=3, concat_axis=2, tiled=True)  45.9 us
    all_to_all x1, waiting for transfers between devices, on_device(): lax.all_to_all(wave_values[1], 'grid', split_axis=2, concat_axis=3, tiled...  45.5 us
    all_to_all x1, waiting for transfers between devices, on_device(): lax.all_to_all(wave_values[0], 'grid', split_axis=2, concat_axis=3, tiled...  40 us
    all_to_all x1, waiting for transfers between devices, on_device(): lax.all_to_all(fields[0], 'grid', split_axis=3, concat_axis=2, tiled=True)  39.8 us
    ppermute x7, waiting for transfers between devices, replace_the_steps_all(): lax.ppermute(raw_out, chip_axis, [(s, s ^ m) for s in range(row_out)])  34.5 us
    all_to_all x1, waiting for transfers between devices, potential_whole(): lax.all_to_all(wave_values[1], 'grid', split_axis=1, concat_axis=0, tiled...  24.4 us
  transfers between devices with their start and end apart: 15, of which 10 were waited for; matrix products, arithmetic and copies ran while one was open for 6% of the time, Pallas kernels for 0%

profile of v1, /device:TPU:0, one launch (start us, length us, event | category | flops | bytes accessed | tf_op | source)
XLA Modules:
  0.0 492.4 jit_solution(8223370783388100206)
XLA Ops:
  6.5 2.5 fusion.381
  9.1 2.6 fusion.18
  11.7 2.6 fusion.19
  14.3 2.6 fusion.25
  16.9 2.6 fusion.24
  19.5 2.4 fusion.12
  21.9 2.1 subtract_bitcast_fusion.3
  24.0 2.6 copy.35
  26.6 7.3 %all-to-all-start = ((f32[1,2,128,16,128]{4,3,1,0,2:T(8,128)}), f32[1,2,128,16,128]{4,3,1,0,2:T(8,128)}, u32[]{:S(2)}, u32[]{:S(2)}) async-start(f32[1,2,128,16,128]{4,3,1,0,2:T(8,128)} %copy.35), calls=%async_computation | async-start | bytes 4194304 | tf_op jit(solution)/shard_map/all_to_all | solution.py:116
  33.8 3.7 fusion.10
  39.7 2.5 copy.39
  42.2 40.0 %all-to-all-done = f32[1,2,128,16,128]{4,3,1,0,2:T(8,128)} async-done(((f32[1,2,128,16,128]{4,3,1,0,2:T(8,128)}), f32[1,2,128,16,128]{4,3,1,0,2:T(8,128)}, u32[]{:S(2)}, u32[]{:S(2)}) %all-to-all-start) | async-done | bytes 2097184 | tf_op jit(solution)/shard_map/all_to_all | solution.py:116
  82.2 4.4 all-to-all-start.1
  88.9 45.5 %all-to-all-done.1 = f32[1,2,128,16,128]{4,3,1,0,2:T(8,128)} async-done(((f32[1,2,128,16,128]{4,3,1,0,2:T(8,128)}), f32[1,2,128,16,128]{4,3,1,0,2:T(8,128)}, u32[]{:S(2)}, u32[]{:S(2)}) %all-to-all-start.1) | async-done | bytes 2097184 | tf_op jit(solution)/shard_map/all_to_all | solution.py:117
  136.2 2.1 fusion.123
  138.3 2.1 fusion.125
  140.5 2.3 add_bitcast_fusion.2
  142.8 2.3 subtract_bitcast_fusion.2
  146.9 50.8 %all-reduce.3.cloned.1.call-done = (f32[16,128,128]{2,1,0:T(8,128)}, f32[16,128,128]{2,1,0:T(8,128)}) async-done(((f32[16,128,128]{2,1,0:T(8,128)}, f32[16,128,128]{2,1,0:T(8,128)}), (f32[16,128,128]{2,1,0:T(8,128)}, f32[16,128,128]{2,1,0:T(8,128)})) %all-reduce.3.cloned.1.call-update) | async-done | bytes 2097168 | tf_op jit(solution)/shard_map/psum | solution.py:122
  197.7 2.6 fusion.111
  208.5 5.5 %all-to-all-start.2 = ((f32[16,128,128]{2,0,1:T(8,128)}), f32[16,128,128]{2,0,1:T(8,128)}, u32[]{:S(2)}, u32[]{:S(2)}) async-start(f32[16,128,128]{2,0,1:T(8,128)} %copy.43), calls=%async_computation.2 | async-start | bytes 2097152 | tf_op jit(solution)/shard_map/all_to_all | solution.py:73
  218.0 21.7 %all-to-all-done.2 = f32[16,128,128]{2,0,1:T(8,128)} async-done(((f32[16,128,128]{2,0,1:T(8,128)}), f32[16,128,128]{2,0,1:T(8,128)}, u32[]{:S(2)}, u32[]{:S(2)}) %all-to-all-start.2) | async-done | bytes 1048608 | tf_op jit(solution)/shard_map/all_to_all | solution.py:73
  239.8 3.8 all-to-all-start.3
  245.1 24.4 %all-to-all-done.3 = f32[16,128,128]{2,0,1:T(8,128)S(1)} async-done(((f32[16,128,128]{2,0,1:T(8,128)}), f32[16,128,128]{2,0,1:T(8,128)S(1)}, u32[]{:S(2)}, u32[]{:S(2)}) %all-to-all-start.3) | async-done | bytes 1048608 | tf_op jit(solution)/shard_map/all_to_all | solution.py:74
  283.5 4.7 all-to-all-start.4
  288.2 4.7 collective-permute-start.6
  297.3 20.8 %collective-permute-done.1 = f32[16,16,128]{2,0,1:T(8,128)S(1)} collective-permute-done((f32[16,16,128]{2,0,1:T(8,128)S(1)}, f32[16,16,128]{2,0,1:T(8,128)S(1)}, u32[]{:S(2)}, u32[]{:S(2)}) %collective-permute-start.1) | collective-permute-done | bytes 131104 | tf_op jit(solution)/shard_map/ppermute | solution.py:96
  318.1 3.6 collective-permute-start.2
  321.7 4.5 collective-permute-done.2
  326.2 9.2 %collective-permute-done.3 = f32[16,16,128]{2,0,1:T(8,128)S(1)} collective-permute-done((f32[16,16,128]{2,0,1:T(8,128)S(1)}, f32[16,16,128]{2,0,1:T(8,128)S(1)}, u32[]{:S(2)}, u32[]{:S(2)}) %collective-permute-start.3) | collective-permute-done | bytes 131104 | tf_op jit(solution)/shard_map/ppermute | solution.py:96
  346.8 2.3 fusion
  349.2 2.1 fusion.1
  352.7 2.3 multiply_add_fusion
  355.0 2.3 multiply_subtract_fusion
  357.3 2.1 fusion.4
  359.5 2.1 subtract_bitcast_fusion.1
  361.6 2.8 copy.58
  364.4 4.3 all-to-all-start.5
  368.7 3.7 fusion.2
  372.4 2.1 add_bitcast_fusion.1
  374.6 2.5 copy.62
  377.1 39.8 %all-to-all-done.5 = f32[1,2,16,128,128]{4,2,1,0,3:T(8,128)} async-done(((f32[1,2,16,128,128]{4,2,1,0,3:T(8,128)}), f32[1,2,16,128,128]{4,2,1,0,3:T(8,128)}, u32[]{:S(2)}, u32[]{:S(2)}) %all-to-all-start.5) | async-done | bytes 2097184 | tf_op jit(solution)/shard_map/all_to_all | solution.py:129
  416.9 4.6 all-to-all-start.6
  423.4 45.9 %all-to-all-done.6 = f32[1,2,16,128,128]{4,2,1,0,3:T(8,128)} async-done(((f32[1,2,16,128,128]{4,2,1,0,3:T(8,128)}), f32[1,2,16,128,128]{4,2,1,0,3:T(8,128)}, u32[]{:S(2)}, u32[]{:S(2)}) %all-to-all-start.6) | async-done | bytes 2097184 | tf_op jit(solution)/shard_map/all_to_all | solution.py:130
  471.2 2.1 fusion.117
  475.5 2.3 add_bitcast_fusion
  477.8 2.3 subtract_bitcast_fusion
  480.6 4.4 copy.64
  (81 shorter events, 59.0 us)
Async XLA Ops:
  19.5 2.4 copy-start.1
  26.6 55.6 %all-to-all-start = ((f32[1,2,128,16,128]{4,3,1,0,2:T(8,128)}), f32[1,2,128,16,128]{4,3,1,0,2:T(8,128)}, u32[]{:S(2)}, u32[]{:S(2)}) async-start(f32[1,2,128,16,128]{4,3,1,0,2:T(8,128)} %copy.35), calls=%async_computation | async-start | bytes 4194304 | tf_op jit(solution)/shard_map/all_to_all | solution.py:116
  82.2 52.2 %all-to-all-start.1 = ((f32[1,2,128,16,128]{4,3,1,0,2:T(8,128)}), f32[1,2,128,16,128]{4,3,1,0,2:T(8,128)}, u32[]{:S(2)}, u32[]{:S(2)}) async-start(f32[1,2,128,16,128]{4,3,1,0,2:T(8,128)} %copy.39), calls=%async_computation.1 | async-start | bytes 4194304 | tf_op jit(solution)/shard_map/all_to_all | solution.py:117
  86.5 111.2 %all-reduce.3.cloned.1.call-start = ((), (), s32[]{:S(2)}) async-start(), calls=%async_computation.7 | async-start | bytes 4194304 | tf_op jit(solution)/shard_map/psum | solution.py:122
  142.7 2.3 copy-start.5
  197.7 2.6 copy-start.2
  201.6 2.7 copy-start.3
  208.5 31.3 %all-to-all-start.2 = ((f32[16,128,128]{2,0,1:T(8,128)}), f32[16,128,128]{2,0,1:T(8,128)}, u32[]{:S(2)}, u32[]{:S(2)}) async-start(f32[16,128,128]{2,0,1:T(8,128)} %copy.43), calls=%async_computation.2 | async-start | bytes 2097152 | tf_op jit(solution)/shard_map/all_to_all | solution.py:73
  239.8 29.7 %all-to-all-start.3 = ((f32[16,128,128]{2,0,1:T(8,128)}), f32[16,128,128]{2,0,1:T(8,128)S(1)}, u32[]{:S(2)}, u32[]{:S(2)}) async-start(f32[16,128,128]{2,0,1:T(8,128)} %copy.47), calls=%async_computation.3 | async-start | bytes 2097152 | tf_op jit(solution)/shard_map/all_to_all | solution.py:74
  279.2 16.7 %collective-permute-start = (f32[16,16,128]{2,0,1:T(8,128)S(1)}, f32[16,16,128]{2,0,1:T(8,128)S(1)}, u32[]{:S(2)}, u32[]{:S(2)}) collective-permute-start(f32[16,16,128]{2,0,1:T(8,128)S(1)} %get-tuple-element.15), channel_id=1, source_target_pairs={{0,1},{1,0},{2,3},{3,2},{4,5},{5,4},{6,7},{7,6},{8,9},{9,8},{10,11... | collective-permute-start | bytes 393224 | tf_op jit(solution)/shard_map/ppermute | solution.py:96
  283.5 54.2 %all-to-all-start.4 = ((f32[128,16,128]{2,1,0:T(8,128)}), f32[128,16,128]{2,1,0:T(8,128)}, u32[]{:S(2)}, u32[]{:S(2)}) async-start(f32[128,16,128]{2,1,0:T(8,128)} %copy.49), calls=%async_computation.4 | async-start | bytes 2097152 | tf_op jit(solution)/shard_map/all_to_all | solution.py:103
  288.2 47.3 %collective-permute-start.6 = (f32[16,16,128]{2,0,1:T(8,128)S(1)}, f32[16,16,128]{2,0,1:T(8,128)S(1)}, u32[]{:S(2)}, u32[]{:S(2)}) collective-permute-start(f32[16,16,128]{2,0,1:T(8,128)S(1)} %get-tuple-element.9), channel_id=1, source_target_pairs={{0,7},{1,6},{2,5},{3,4},{4,3},{5,2},{6,1},{7,0},{8,15},{9,14},{10,... | collective-permute-start | bytes 393224 | tf_op jit(solution)/shard_map/ppermute | solution.py:96
  292.9 42.6 %collective-permute-start.5 = (f32[16,16,128]{2,0,1:T(8,128)S(1)}, f32[16,16,128]{2,0,1:T(8,128)S(1)}, u32[]{:S(2)}, u32[]{:S(2)}) collective-permute-start(f32[16,16,128]{2,0,1:T(8,128)S(1)} %get-tuple-element.10), channel_id=1, source_target_pairs={{0,6},{1,7},{2,4},{3,5},{4,2},{5,3},{6,0},{7,1},{8,14},{9,15},{10,... | collective-permute-start | bytes 393224 | tf_op jit(solution)/shard_map/ppermute | solution.py:96
  293.4 42.0 %collective-permute-start.4 = (f32[16,16,128]{2,0,1:T(8,128)S(1)}, f32[16,16,128]{2,0,1:T(8,128)S(1)}, u32[]{:S(2)}, u32[]{:S(2)}) collective-permute-start(f32[16,16,128]{2,0,1:T(8,128)S(1)} %get-tuple-element.11), channel_id=1, source_target_pairs={{0,5},{1,4},{2,7},{3,6},{4,1},{5,0},{6,3},{7,2},{8,13},{9,12},{10,... | collective-permute-start | bytes 393224 | tf_op jit(solution)/shard_map/ppermute | solution.py:96
  294.0 41.4 %collective-permute-start.3 = (f32[16,16,128]{2,0,1:T(8,128)S(1)}, f32[16,16,128]{2,0,1:T(8,128)S(1)}, u32[]{:S(2)}, u32[]{:S(2)}) collective-permute-start(f32[16,16,128]{2,0,1:T(8,128)S(1)} %get-tuple-element.12), channel_id=1, source_target_pairs={{0,4},{1,5},{2,6},{3,7},{4,0},{5,1},{6,2},{7,3},{8,12},{9,13},{10,... | collective-permute-start | bytes 393224 | tf_op jit(solution)/shard_map/ppermute | solution.py:96
  295.9 22.2 %collective-permute-start.1 = (f32[16,16,128]{2,0,1:T(8,128)S(1)}, f32[16,16,128]{2,0,1:T(8,128)S(1)}, u32[]{:S(2)}, u32[]{:S(2)}) collective-permute-start(f32[16,16,128]{2,0,1:T(8,128)S(1)} %get-tuple-element.14), channel_id=1, source_target_pairs={{0,2},{1,3},{2,0},{3,1},{4,6},{5,7},{6,4},{7,5},{8,10},{9,11},{10,... | collective-permute-start | bytes 393224 | tf_op jit(solution)/shard_map/ppermute | solution.py:96
  318.1 8.1 %collective-permute-start.2 = (f32[16,16,128]{2,0,1:T(8,128)S(1)}, f32[16,16,128]{2,0,1:T(8,128)S(1)}, u32[]{:S(2)}, u32[]{:S(2)}) collective-permute-start(f32[16,16,128]{2,0,1:T(8,128)S(1)} %get-tuple-element.13), channel_id=1, source_target_pairs={{0,3},{1,2},{2,1},{3,0},{4,7},{5,6},{6,5},{7,4},{8,11},{9,10},{10,... | collective-permute-start | bytes 393224 | tf_op jit(solution)/shard_map/ppermute | solution.py:96
  343.0 2.5 copy-start.4
  343.0 2.5 copy-start.6
  343.0 2.5 copy-start.7
  357.3 2.2 copy-start
  364.4 52.6 %all-to-all-start.5 = ((f32[1,2,16,128,128]{4,2,1,0,3:T(8,128)}), f32[1,2,16,128,128]{4,2,1,0,3:T(8,128)}, u32[]{:S(2)}, u32[]{:S(2)}) async-start(f32[1,2,16,128,128]{4,2,1,0,3:T(8,128)} %copy.58), calls=%async_computation.5 | async-start | bytes 4194304 | tf_op jit(solution)/shard_map/all_to_all | solution.py:129
  416.9 52.4 %all-to-all-start.6 = ((f32[1,2,16,128,128]{4,2,1,0,3:T(8,128)}), f32[1,2,16,128,128]{4,2,1,0,3:T(8,128)}, u32[]{:S(2)}, u32[]{:S(2)}) async-start(f32[1,2,16,128,128]{4,2,1,0,3:T(8,128)} %copy.62), calls=%async_computation.6 | async-start | bytes 4194304 | tf_op jit(solution)/shard_map/all_to_all | solution.py:130
Sparse Core Ops, SparseCore 0:
  147.0 50.6 all-reduce.2
